TPU v7x, 512 devices: a whole 4x8x8 slice. The times are simulated.
512 devices in a mesh: dp: 64 (over z_hi, y, core), tensor: 8 (over z_lo, x).
Axes of the slice: x: 4, y: 8, z: 8 (z_hi: 4, z_lo: 2; z = z_hi * 2 + z_lo), core: 2. Of those that a mesh axis runs over, the one named last changes fastest.
Arguments:
- tokens: bfloat16 [32768, 8192], P('dp', 'tensor'), may hold values from -6 to 6
- value_weight: bfloat16 [8192, 1024], P('tensor', 'dp'), may hold values from -0.0625 to 0.0625
- adapter_down_weights: bfloat16 [8, 8192, 64], P(None, 'tensor'), may hold values from -0.0625 to 0.0625
- adapter_up_weights: bfloat16 [8, 64, 1024], P(None, None, 'tensor'), may hold values from -0.75 to 0.75
- value_gradient: bfloat16 [32768, 1024], P(('dp', 'tensor')), may hold values from -12 to 12
- block_adapter_index: int32 [256, 1], replicated, may hold values from 0 to 7
- block_live_rows: int32 [256], replicated, may hold values from 1 to 128
Outputs:
- values_out: bfloat16 [32768, 1024], P(('dp', 'tensor'))
- input_gradient: bfloat16 [32768, 8192], P('dp', 'tensor')
- grad_a: float32 [8, 8192, 64], P(None, 'tensor')
- grad_b: float32 [8, 64, 1024], P(None, None, 'tensor')
Inputs may be any that keep to these rules, and one draw needn't show every extreme that they name: `block_adapter_index`: every adapter names at least one block.
All inputs are finite; a program needn't handle non-finite values.
Results may differ from a plain program's by a relative error of at most 0.02.
Values may be sent and summed in bfloat16 or wider, within the bound.
No kernel may reach another device: no remote copies, remote signals or barrier semaphores. Data moves between devices by JAX's collectives and lax.ppermute only.
A program may use at most 64 MiB of HBM per device.

v0:
```python
import jax
import jax.numpy as jnp
from jax import lax
from jax.sharding import PartitionSpec as P

BLK = 128
ADAPTER_SCALE = 2.0


def shards(
    tokens,
    value_weight,
    adapter_down_weights,
    adapter_up_weights,
    value_gradient,
    block_adapter_index,
    block_live_rows,
):
    local_rows = tokens.shape[0]
    tensor_size = lax.axis_size("tensor")
    own_rows = local_rows // tensor_size
    data_index = lax.axis_index("dp")
    tensor_index = lax.axis_index("tensor")
    adapter_count = adapter_down_weights.shape[0]
    local_width = tokens.shape[1]
    rank_columns = adapter_down_weights.shape[2]
    head_columns = adapter_up_weights.shape[2]
    local_blocks = local_rows // BLK
    all_ids = block_adapter_index[:, 0]
    block_indices = lax.dynamic_slice_in_dim(all_ids, data_index * local_blocks, local_blocks)
    block_fill = lax.dynamic_slice_in_dim(block_live_rows, data_index * local_blocks, local_blocks)
    adapter_range = jnp.arange(adapter_count, dtype=jnp.int32)
    block_onehot = (block_indices[:, None] == adapter_range[None, :]).astype(jnp.float32)
    complete_up_weight = lax.all_gather(adapter_up_weights, "tensor", axis=2, tiled=True)
    up_flat = complete_up_weight.reshape(adapter_count * rank_columns, complete_up_weight.shape[2])
    selected_down_weight = adapter_down_weights[block_indices]
    token_block_rows = tokens.reshape(local_blocks, BLK, local_width)
    reduced_part = jnp.einsum(
        "cpe,cev->cpv", token_block_rows, selected_down_weight, preferred_element_type=jnp.float32
    )
    reduced = lax.psum(reduced_part.astype(jnp.bfloat16), "tensor")
    w_full = lax.all_gather(value_weight, "dp", axis=1, tiled=True)
    base_own = lax.psum_scatter(
        jnp.dot(tokens, w_full, preferred_element_type=jnp.float32).astype(jnp.bfloat16),
        "tensor",
        scatter_dimension=0,
        tiled=True,
    ).astype(jnp.float32)
    row_index = tensor_index * own_rows + jnp.arange(own_rows, dtype=jnp.int32)
    row_block = row_index // BLK
    row_ids = block_indices[row_block]
    row_onehot = row_ids[:, None] == adapter_range[None, :]
    reduced_own = lax.dynamic_slice_in_dim(
        reduced.reshape(local_rows, rank_columns), tensor_index * own_rows, own_rows, 0
    )
    spread = (row_onehot[:, :, None].astype(jnp.bfloat16) * reduced_own[:, None, :]).reshape(
        own_rows, adapter_count * rank_columns
    )
    update = jnp.dot(spread, up_flat, preferred_element_type=jnp.float32)
    values_out = (base_own + ADAPTER_SCALE * update).astype(jnp.bfloat16)
    live_rows = row_index % BLK < block_fill[row_block]
    masked = jnp.where(live_rows[:, None], value_gradient, jnp.zeros_like(value_gradient))
    projected = jnp.einsum("kc,mc->km", masked, up_flat, preferred_element_type=jnp.float32)
    grad_low = jnp.sum(
        projected.reshape(own_rows, adapter_count, rank_columns)
        * row_onehot[:, :, None].astype(jnp.float32),
        axis=1,
    ).astype(jnp.bfloat16)
    whole_grad, whole_low = (
        lax.all_gather(masked, "tensor", axis=0, tiled=True),
        lax.all_gather(grad_low, "tensor", axis=0, tiled=True),
    )
    lowrank_block_rows = whole_low.reshape(local_blocks, BLK, rank_columns)
    base_backward = jnp.einsum("kc,dc->kd", whole_grad, w_full, preferred_element_type=jnp.float32)
    adapter_backward = jnp.einsum(
        "sly,say->sla", lowrank_block_rows, selected_down_weight, preferred_element_type=jnp.float32
    ).reshape(local_rows, local_width)
    input_gradient = (base_backward + ADAPTER_SCALE * adapter_backward).astype(jnp.bfloat16)
    down_terms = jnp.einsum(
        "xgj,xgi->xji", token_block_rows, lowrank_block_rows, preferred_element_type=jnp.float32
    )
    down_local = jnp.einsum(
        "ba,bdr->adr", block_onehot, down_terms, precision=lax.Precision.HIGHEST
    )
    grad_cols = lax.dynamic_slice_in_dim(
        whole_grad, tensor_index * head_columns, head_columns, 1
    ).reshape(local_blocks, BLK, head_columns)
    up_terms = jnp.einsum("bkr,bkc->brc", reduced, grad_cols, preferred_element_type=jnp.float32)
    up_local = jnp.einsum("ba,brc->arc", block_onehot, up_terms, precision=lax.Precision.HIGHEST)
    all_onehot = (all_ids[:, None] == adapter_range[None, :]).astype(jnp.float32)
    tallies = jnp.sum(all_onehot * block_live_rows[:, None].astype(jnp.float32), axis=0)
    factor = ADAPTER_SCALE / tallies
    down_sum, up_sum = lax.psum((down_local, up_local), "dp")
    grad_a = down_sum * factor[:, None, None]
    grad_b = up_sum * factor[:, None, None]
    return (values_out, input_gradient, grad_a, grad_b)


def solution(mesh):
    return jax.shard_map(
        shards,
        mesh=mesh,
        in_specs=(
            P("dp", "tensor"),
            P("tensor", "dp"),
            P(None, "tensor", None),
            P(None, None, "tensor"),
            P(("dp", "tensor"), None),
            P(),
            P(),
        ),
        out_specs=(
            P(("dp", "tensor"), None),
            P("dp", "tensor"),
            P(None, "tensor", None),
            P(None, None, "tensor"),
        ),
        check_vma=False,
    )
```

profile of v0, /device:TPU:8, one launch (start us, length us, event | category | flops | bytes accessed | tf_op | source)
XLA Modules:
  0.0 890.9 jit_solution(14993300499443759841)
XLA Ops:
  7.2 0.0 copy-start
  7.2 0.0 all-gather.6.cloned.1.call-start
  7.2 0.7 all-gather.6.cloned.1.call-update
  7.9 0.0 all-gather.8.cloned.1.call-start
  8.0 0.8 dynamic_slice.17
  8.7 0.6 fusion.26
  9.3 2.6 fusion.21
  11.9 1.6 broadcast_select_fusion
  13.6 0.0 copy-start.2
  13.6 0.0 all-gather.8.cloned.1.call-update
  13.6 0.0 all-reduce.4.cloned.1.call-start
  13.6 0.7 fusion.25
  14.4 1.8 gather_fusion
  16.2 0.0 copy-done
  16.2 1.1 fusion.5
  17.3 0.0 all-reduce.4.cloned.1.call-update
  17.3 0.0 all-gather.4.cloned.1.call-start
  17.4 0.5 all-gather.4.cloned.1.call-update
  17.9 0.0 all-reduce.6.cloned.1.call-start
  18.0 0.6 fusion.27
  18.6 2.6 fusion.23
  21.2 36.1 %all-gather.6.cloned.1.call-done = bf16[8,64,1024]{2,1,0:T(8,128)(2,1)} async-done(((bf16[8,64,128]{2,1,0:T(8,128)(2,1)}), bf16[8,64,1024]{2,1,0:T(8,128)(2,1)}) %all-gather.6.cloned.1.call-update) | async-done | bytes 1048592 | tf_op jit(solution)/shard_map/all_gather | solution.py:34
  57.3 0.0 copy-done.2
  57.3 1.9 fusion.4
  59.1 28.3 %all_gather.15 = bf16[512,64]{1,0:T(8,128)(2,1)S(1)} all-gather(bf16[64,64]{1,0:T(8,128)(2,1)S(1)} %fusion.4), channel_id=1, replica_groups=mesh['dp'=64,'tensor'=8] {'tensor'}, dimensions={0}, use_global_device_ids=true | all-gather | bytes 73728 | tf_op jit(solution)/shard_map/all_gather | solution.py:71
  87.4 18.4 %all-gather.8.cloned.1.call-done = bf16[512,1024]{1,0:T(8,128)(2,1)} async-done(((bf16[64,1024]{1,0:T(8,128)(2,1)}), bf16[512,1024]{1,0:T(8,128)(2,1)}) %all-gather.8.cloned.1.call-update) | async-done | bytes 1048592 | tf_op jit(solution)/shard_map/all_gather | solution.py:70
  105.7 0.9 constant_dynamic-slice_fusion
  106.7 85.2 %all-reduce.4.cloned.1.call-done = bf16[4,128,64]{1,2,0:T(8,128)(2,1)} async-done(((bf16[4,128,64]{1,2,0:T(8,128)(2,1)}), bf16[4,128,64]{1,2,0:T(8,128)(2,1)}) %all-reduce.4.cloned.1.call-update) | async-done | bytes 65552 | tf_op jit(solution)/shard_map/psum | solution.py:41
  191.8 1.0 fusion.28
  192.8 1.1 fusion.9
  193.9 0.4 convolution_bitcast_fusion
  194.3 3.2 fusion.6
  197.5 0.0 all-reduce.6.cloned.1.call-update
  197.5 0.0 copy-start.7
  197.5 0.0 copy-start.6
  197.6 0.0 copy-start.4
  197.6 0.0 reduce-scatter.2.cloned.1.call-start
  197.6 81.2 %all-gather.4.cloned.1.call-done = bf16[1024,1024]{0,1:T(8,128)(2,1)} async-done(((bf16[1024,16]{0,1:T(8,128)(2,1)}), bf16[1024,1024]{0,1:T(8,128)(2,1)}) %all-gather.4.cloned.1.call-update) | async-done | bytes 2097168 | tf_op jit(solution)/shard_map/all_gather | solution.py:42
  278.9 3.9 convolution_convert_fusion
  282.7 0.0 copy-start.5
  282.7 0.0 reduce-scatter.2.cloned.1.call-update
  282.7 0.0 copy-done.7
  282.8 0.0 copy-done.6
  282.8 0.1 select_reduce_fusion
  282.9 0.0 copy-done.4
  282.9 0.1 constant_dynamic-slice_fusion.1
  283.0 0.1 copy.28
  283.1 0.0 copy-start.8
  283.1 0.4 convolution_multiply_fusion
  283.5 0.4 copy-done.5
  283.9 0.8 copy-done.8
  284.8 2.2 fusion
  287.0 548.4 %all-reduce.6.cloned.1.call-done = (f32[8,1024,64]{1,0,2:T(8,128)}, f32[8,64,128]{2,0,1:T(8,128)}) async-done(((f32[8,1024,64]{1,0,2:T(8,128)}, f32[8,64,128]{2,0,1:T(8,128)}), (f32[8,1024,64]{1,0,2:T(8,128)}, f32[8,64,128]{2,0,1:T(8,128)})) %all-reduce.6.cloned.1.call-update) | async-done | bytes 2359312 | tf_op jit(solution)/shard_map/psum | solution.py:93
  835.4 1.8 broadcast_multiply_fusion
  837.3 0.0 copy-start.3
  837.3 0.0 copy-start.1
  837.3 2.5 copy.34
  839.8 0.0 copy-done.3
  839.8 0.1 broadcast_multiply_fusion.1
  839.9 0.8 copy.35
  840.7 41.4 %reduce-scatter.2.cloned.1.call-done = bf16[64,1024]{1,0:T(8,128)(2,1)} async-done(((bf16[512,1024]{1,0:T(8,128)(2,1)}), bf16[64,1024]{1,0:T(8,128)(2,1)}) %reduce-scatter.2.cloned.1.call-update) | async-done | bytes 131088 | tf_op jit(solution)/shard_map/reduce_scatter | solution.py:43
  882.1 0.0 copy-done.1
  882.1 2.0 fusion.3
  (5 shorter events, 0.0 us)
Async XLA Ops:
  7.2 9.0 %copy-start = (bf16[512,1024]{1,0:T(8,128)(2,1)S(1)}, bf16[512,1024]{1,0:T(8,128)(2,1)}, u32[]{:S(2)}) copy-start(bf16[512,1024]{1,0:T(8,128)(2,1)} %param.7) | copy-start | bytes 3145732
  7.2 50.1 %all-gather.6.cloned.1.call-start = ((), (), s32[]{:S(2)}) async-start(), calls=%async_computation.4 | async-start | bytes 1179648 | tf_op jit(solution)/shard_map/all_gather | solution.py:34
  7.9 97.8 %all-gather.8.cloned.1.call-start = ((), (), s32[]{:S(2)}) async-start(), calls=%async_computation.5 | async-start | bytes 1179648 | tf_op jit(solution)/shard_map/all_gather | solution.py:70
  13.6 43.7 %copy-start.2 = (bf16[64,1024]{1,0:T(8,128)(2,1)S(1)}, bf16[64,1024]{1,0:T(8,128)(2,1)}, u32[]{:S(2)}) copy-start(bf16[64,1024]{1,0:T(8,128)(2,1)} %broadcast_select_fusion) | copy-start | bytes 393220
  13.6 178.2 %all-reduce.4.cloned.1.call-start = ((), (), s32[]{:S(2)}) async-start(), calls=%async_computation.3 | async-start | bytes 131072 | tf_op jit(solution)/shard_map/psum | solution.py:41
  17.3 261.5 %all-gather.4.cloned.1.call-start = ((), (), s32[]{:S(2)}) async-start(), calls=%async_computation.1 | async-start | bytes 2129920 | tf_op jit(solution)/shard_map/all_gather | solution.py:42
  17.9 817.5 %all-reduce.6.cloned.1.call-start = ((), (), s32[]{:S(2)}) async-start(), calls=%async_computation.6 | async-start | bytes 4718592 | tf_op jit(solution)/shard_map/psum | solution.py:93
  197.5 85.2 %copy-start.7 = (s32[256]{0:T(256)S(1)}, s32[256]{0:T(256)}, u32[]{:S(2)}) copy-start(s32[256]{0:T(256)} %param.13) | copy-start | bytes 3076
  197.5 85.2 %copy-start.6 = (s32[256,1]{0,1:T(1,128)S(1)}, s32[256,1]{0,1:T(1,128)}, u32[]{:S(2)}) copy-start(s32[256,1]{0,1:T(1,128)} %param.12) | copy-start | bytes 3076
  197.6 85.4 %copy-start.4 = (bf16[4,128,64]{1,2,0:T(8,128)(2,1)S(1)}, bf16[4,128,64]{1,2,0:T(8,128)(2,1)}, u32[]{:S(2)}) copy-start(bf16[4,128,64]{1,2,0:T(8,128)(2,1)} %all-reduce.4.cloned.1.call-done) | copy-start | bytes 196612
  197.6 684.5 %reduce-scatter.2.cloned.1.call-start = ((), (), s32[]{:S(2)}) async-start(), calls=%async_computation.2 | async-start | bytes 1179648 | tf_op jit(solution)/shard_map/reduce_scatter | solution.py:43
  282.7 1.2 copy-start.5
  283.1 1.7 copy-start.8
  837.3 2.6 copy-start.3
  837.3 44.8 %copy-start.1 = (bf16[8,64,1024]{2,1,0:T(8,128)(2,1)S(1)}, bf16[8,64,1024]{2,1,0:T(8,128)(2,1)}, u32[]{:S(2)}) copy-start(bf16[8,64,1024]{2,1,0:T(8,128)(2,1)} %all-gather.6.cloned.1.call-done) | copy-start | bytes 3145732
Sparse Core Ops, SparseCore 0:
  10.0 47.1 all-gather.5
  59.9 45.7 all-gather.7
  109.2 82.5 all-reduce.3
  195.6 83.2 all-gather.3
  282.5 552.8 all-reduce.5
  838.1 43.9 reduce-scatter.1
where the time goes:
time: 891 us
  waiting for transfers between devices  812 us (91%)
  blocking collectives  28.3 us (3%)
  matrix products  17.1 us (2%)
  between operations  14.3 us (2%)
  other arithmetic  9.62 us (1%)
  local copies, waits for them, and re-layouts  9.44 us (1%)
    psum x1, waiting for transfers between devices, shards(): down_sum, up_sum = lax.psum((down_local, up_local), 'dp')  548 us
    psum x1, waiting for transfers between devices, shards(): reduced = lax.psum(reduced_part.astype(jnp.bfloat16), 'tensor')  85.2 us
    all_gather x1, waiting for transfers between devices, shards(): w_full = lax.all_gather(value_weight, 'dp', axis=1, tiled=True)  81.2 us
    reduce_scatter x1, waiting for transfers between devices, shards(): lax.psum_scatter(jnp.dot(tokens, w_full, preferred_element_type=jnp.float...  41.4 us
    all_gather x1, waiting for transfers between devices, shards(): lax.all_gather(adapter_up_weights, 'tensor', axis=2, tiled=True)  36.1 us
    all_gather x1, blocking collectives, shards(): lax.all_gather(grad_low, 'tensor', axis=0, tiled=True)  28.3 us
    all_gather x1, waiting for transfers between devices, shards(): lax.all_gather(masked, 'tensor', axis=0, tiled=True)  18.4 us
  transfers between devices with their start and end apart: 6, of which 6 were waited for; matrix products, arithmetic and copies ran while one was open for 4% of the time, Pallas kernels for 0%

commit v1 on v0

--- a/solution.py
+++ b/solution.py
@@ -38,7 +38,7 @@
     reduced_part = jnp.einsum(
         "cpe,cev->cpv", token_block_rows, selected_down_weight, preferred_element_type=jnp.float32
     )
-    reduced = lax.psum(reduced_part.astype(jnp.bfloat16), "tensor")
+    reduced = jnp.sum(lax.all_gather(reduced_part.astype(jnp.bfloat16), "tensor"), axis=0)
     w_full = lax.all_gather(value_weight, "dp", axis=1, tiled=True)
     base_own = lax.psum_scatter(
         jnp.dot(tokens, w_full, preferred_element_type=jnp.float32).astype(jnp.bfloat16),

time: 891 us -> 806 us (0.905)
  waiting for transfers between devices: 812 us -> 697 us
  blocking collectives: 28.3 us -> 59.3 us
    psum x1 -> x0, waiting for transfers between devices: 85.2 us -> none  [shards(): reduced = lax.psum(reduced_part.astype(jnp.bfloat16), 'tensor')]
    all_gather x0 -> x1, blocking collectives: none -> 30.8 us  [shards(): lax.all_gather(reduced_part.astype(jnp.bfloat16), 'tensor')]
    all_gather x1, waiting for transfers between devices: 36.1 us -> 6.64 us  [shards(): lax.all_gather(adapter_up_weights, 'tensor', axis=2, tiled=True)]
  transfers between devices with their start and end apart: 6 -> 5, of which waited for: 6 -> 5; matrix products, arithmetic and copies ran while one was open for 4% -> 4% of each run, Pallas kernels for 0% -> 0%
where the time goes in v1:
time: 806 us; the launch traced here: 805 us
  waiting for transfers between devices  697 us (86%)
  blocking collectives  59.3 us (7%)
  matrix products  15.7 us (2%)
  between operations  13.9 us (2%)
  other arithmetic  9.69 us (1%)
  local copies, waits for them, and re-layouts  9.37 us (1%)
    psum x1, waiting for transfers between devices, shards(): down_sum, up_sum = lax.psum((down_local, up_local), 'dp')  548 us
    all_gather x1, waiting for transfers between devices, shards(): w_full = lax.all_gather(value_weight, 'dp', axis=1, tiled=True)  80.6 us
    reduce_scatter x1, waiting for transfers between devices, shards(): lax.psum_scatter(jnp.dot(tokens, w_full, preferred_element_type=jnp.float...  41.6 us
    all_gather x1, blocking collectives, shards(): lax.all_gather(reduced_part.astype(jnp.bfloat16), 'tensor')  30.8 us
    all_gather x1, blocking collectives, shards(): lax.all_gather(grad_low, 'tensor', axis=0, tiled=True)  28.5 us
    all_gather x1, waiting for transfers between devices, shards(): lax.all_gather(masked, 'tensor', axis=0, tiled=True)  18.5 us
  transfers between devices with their start and end apart: 5, of which 5 were waited for; matrix products, arithmetic and copies ran while one was open for 4% of the time, Pallas kernels for 0%

profile of v1, /device:TPU:8, one launch (start us, length us, event | category | flops | bytes accessed | tf_op | source)
XLA Modules:
  0.0 805.2 jit_solution(5225676751857999779)
XLA Ops:
  7.2 0.0 copy-start
  7.2 0.0 all-gather.7.cloned.1.call-start
  7.2 0.7 all-gather.7.cloned.1.call-update
  7.9 0.0 all-gather.9.cloned.1.call-start
  8.0 0.8 dynamic_slice.17
  8.7 0.6 fusion.26
  9.3 2.6 fusion.21
  11.9 1.6 broadcast_select_fusion
  13.6 0.0 all-gather.9.cloned.1.call-update
  13.6 0.0 all-gather.5.cloned.1.call-start
  13.6 0.7 all-gather.5.cloned.1.call-update
  14.3 0.0 all-reduce.3.cloned.1.call-start
  14.4 0.7 fusion.25
  15.1 0.0 copy-start.2
  15.1 1.8 gather_fusion
  17.0 0.0 copy-done
  17.0 0.5 fusion.5
  17.5 30.8 %all-gather = bf16[32,128,64]{1,2,0:T(8,128)(2,1)S(1)} all-gather(bf16[4,128,64]{1,2,0:T(8,128)(2,1)S(1)} %fusion.5), channel_id=2, replica_groups=mesh['dp'=64,'tensor'=8] {'tensor'}, dimensions={0}, use_global_device_ids=true | all-gather | bytes 589824 | tf_op jit(solution)/shard_map/all_gather | solution.py:41
  48.3 0.1 reduce_sum.30
  48.4 0.6 fusion.27
  49.0 2.6 fusion.23
  51.5 6.6 all-gather.7.cloned.1.call-done
  58.2 0.0 copy-done.2
  58.2 1.9 fusion.4
  60.0 28.5 %all_gather.23 = bf16[512,64]{1,0:T(8,128)(2,1)S(1)} all-gather(bf16[64,64]{1,0:T(8,128)(2,1)S(1)} %fusion.4), channel_id=1, replica_groups=mesh['dp'=64,'tensor'=8] {'tensor'}, dimensions={0}, use_global_device_ids=true | all-gather | bytes 73728 | tf_op jit(solution)/shard_map/all_gather | solution.py:71
  88.5 18.5 %all-gather.9.cloned.1.call-done = bf16[512,1024]{1,0:T(8,128)(2,1)} async-done(((bf16[64,1024]{1,0:T(8,128)(2,1)}), bf16[512,1024]{1,0:T(8,128)(2,1)}) %all-gather.9.cloned.1.call-update) | async-done | bytes 1048592 | tf_op jit(solution)/shard_map/all_gather | solution.py:70
  107.1 0.9 constant_dynamic-slice_fusion
  108.0 0.1 fusion.28
  108.1 1.1 fusion.9
  109.3 0.3 convolution_bitcast_fusion
  109.6 3.2 fusion.6
  112.8 0.0 all-reduce.3.cloned.1.call-update
  112.8 0.0 copy-start.6
  112.9 0.0 copy-start.5
  112.9 0.0 reduce-scatter.2.cloned.1.call-start
  112.9 80.6 %all-gather.5.cloned.1.call-done = bf16[1024,1024]{0,1:T(8,128)(2,1)} async-done(((bf16[1024,16]{0,1:T(8,128)(2,1)}), bf16[1024,1024]{0,1:T(8,128)(2,1)}) %all-gather.5.cloned.1.call-update) | async-done | bytes 2097168 | tf_op jit(solution)/shard_map/all_gather | solution.py:42
  193.5 3.9 convolution_convert_fusion
  197.4 0.0 copy-start.4
  197.4 0.0 reduce-scatter.2.cloned.1.call-update
  197.4 0.0 copy-done.6
  197.5 0.1 constant_dynamic-slice_fusion.1
  197.6 0.1 copy.33
  197.7 0.0 copy-start.7
  197.7 0.0 copy-done.5
  197.7 0.1 select_reduce_fusion
  197.8 0.4 convolution_multiply_fusion
  198.2 0.4 copy-done.4
  198.6 0.8 copy-done.7
  199.4 2.2 fusion
  201.6 548.2 %all-reduce.3.cloned.1.call-done = (f32[8,1024,64]{1,0,2:T(8,128)}, f32[8,64,128]{2,0,1:T(8,128)}) async-done(((f32[8,1024,64]{1,0,2:T(8,128)}, f32[8,64,128]{2,0,1:T(8,128)}), (f32[8,1024,64]{1,0,2:T(8,128)}, f32[8,64,128]{2,0,1:T(8,128)})) %all-reduce.3.cloned.1.call-update) | async-done | bytes 2359312 | tf_op jit(solution)/shard_map/psum | solution.py:93
  749.8 1.8 broadcast_multiply_fusion
  751.7 0.0 copy-start.3
  751.7 0.0 copy-start.1
  751.7 2.5 copy.39
  754.2 0.0 copy-done.3
  754.2 0.1 broadcast_multiply_fusion.1
  754.3 0.8 copy.40
  755.1 41.6 %reduce-scatter.2.cloned.1.call-done = bf16[64,1024]{1,0:T(8,128)(2,1)} async-done(((bf16[512,1024]{1,0:T(8,128)(2,1)}), bf16[64,1024]{1,0:T(8,128)(2,1)}) %reduce-scatter.2.cloned.1.call-update) | async-done | bytes 131088 | tf_op jit(solution)/shard_map/reduce_scatter | solution.py:43
  796.7 0.0 copy-done.1
  796.7 2.0 fusion.3
  (5 shorter events, 0.0 us)
Async XLA Ops:
  7.2 9.8 %copy-start = (bf16[512,1024]{1,0:T(8,128)(2,1)S(1)}, bf16[512,1024]{1,0:T(8,128)(2,1)}, u32[]{:S(2)}) copy-start(bf16[512,1024]{1,0:T(8,128)(2,1)} %param.7) | copy-start | bytes 3145732
  7.2 51.0 %all-gather.7.cloned.1.call-start = ((), (), s32[]{:S(2)}) async-start(), calls=%async_computation.3 | async-start | bytes 1179648 | tf_op jit(solution)/shard_map/all_gather | solution.py:34
  7.9 99.1 %all-gather.9.cloned.1.call-start = ((), (), s32[]{:S(2)}) async-start(), calls=%async_computation.4 | async-start | bytes 1179648 | tf_op jit(solution)/shard_map/all_gather | solution.py:70
  13.6 179.9 %all-gather.5.cloned.1.call-start = ((), (), s32[]{:S(2)}) async-start(), calls=%async_computation.1 | async-start | bytes 2129920 | tf_op jit(solution)/shard_map/all_gather | solution.py:42
  14.3 735.5 %all-reduce.3.cloned.1.call-start = ((), (), s32[]{:S(2)}) async-start(), calls=%async_computation.5 | async-start | bytes 4718592 | tf_op jit(solution)/shard_map/psum | solution.py:93
  15.1 43.1 %copy-start.2 = (bf16[64,1024]{1,0:T(8,128)(2,1)S(1)}, bf16[64,1024]{1,0:T(8,128)(2,1)}, u32[]{:S(2)}) copy-start(bf16[64,1024]{1,0:T(8,128)(2,1)} %broadcast_select_fusion) | copy-start | bytes 393220
  112.8 84.6 %copy-start.6 = (s32[256]{0:T(256)S(1)}, s32[256]{0:T(256)}, u32[]{:S(2)}) copy-start(s32[256]{0:T(256)} %param.13) | copy-start | bytes 3076
  112.9 84.8 %copy-start.5 = (s32[256,1]{0,1:T(1,128)S(1)}, s32[256,1]{0,1:T(1,128)}, u32[]{:S(2)}) copy-start(s32[256,1]{0,1:T(1,128)} %param.12) | copy-start | bytes 3076
  112.9 683.8 %reduce-scatter.2.cloned.1.call-start = ((), (), s32[]{:S(2)}) async-start(), calls=%async_computation.2 | async-start | bytes 1179648 | tf_op jit(solution)/shard_map/reduce_scatter | solution.py:43
  197.4 1.2 copy-start.4
  197.7 1.7 copy-start.7
  751.7 2.6 copy-start.3
  751.7 45.0 %copy-start.1 = (bf16[8,64,1024]{2,1,0:T(8,128)(2,1)S(1)}, bf16[8,64,1024]{2,1,0:T(8,128)(2,1)}, u32[]{:S(2)}) copy-start(bf16[8,64,1024]{2,1,0:T(8,128)(2,1)} %all-gather.7.cloned.1.call-done) | copy-start | bytes 3145732
Sparse Core Ops, SparseCore 0:
  10.0 48.1 all-gather.6
  60.8 46.1 all-gather.8
  110.4 83.0 all-gather.4
  197.0 552.8 all-reduce.2
  752.7 43.9 reduce-scatter.1
